TPU v7x, 128 devices: a whole 4x4x4 slice. The times are simulated.
128 devices in a mesh: row: 8 (over y_hi, x), feat: 16 (over y_lo, z, core).
Axes of the slice: x: 4, y: 4 (y_hi: 2, y_lo: 2; y = y_hi * 2 + y_lo), z: 4, core: 2. Of those that a mesh axis runs over, the one named last changes fastest.
Arguments:
- design_tiles: bfloat16 [8, 8, 8, 48, 128, 128], P('row', None, None, 'feat'), may hold values from -0.078125 to 0.078125
- block_ids: int32 [8, 8, 8, 48], P(None, None, None, 'feat'), may hold values from 0 to 1023, as said below
- responses: bfloat16 [8, 8, 8, 128, 64], P('row'), may hold values from -6 to 6
- live_groups: int32 [8, 8], replicated, may hold values from 0 to 1, as said below
- start_coef: float32 [131072, 64], P('feat'), may hold values from -6 to 6
Outputs:
- coefficients: float32 [131072, 64], P('feat')
Inputs may be any that keep to these rules, and one draw needn't show every extreme that they name: `block_ids`: the 3 entries of a row block that lie in feat index f's positions are distinct feature blocks of the range f * 64 to (f + 1) * 64 - 1. `live_groups`: A group is all live or all empty; every owner has live groups from exactly half of the 8 sources.
All inputs are finite; a program needn't handle non-finite values.
Results may differ from a plain program's by a relative error of at most 0.002.
Values may be sent and summed in bfloat16 or wider, within the bound.
No kernel may reach another device: no remote copies, remote signals or barrier semaphores. Data moves between devices by JAX's collectives and lax.ppermute only.
A program may use at most 64 MiB of HBM per device.

v0:
```python
import jax
import jax.numpy as jnp
from jax import lax
from jax.sharding import PartitionSpec as P

ITERS = 2
step_size = 0.25
ridge_term = 0.05


def huber_weights(predicted, work_resp, live_flags):
    groups, slot_count, block_rows, columns = predicted.shape
    threshold = 1.4 * columns**0.5
    totals = lax.psum(predicted, "feat")
    residual = work_resp.astype(jnp.float32) - totals
    row_norms = jnp.sqrt(jnp.sum(residual * residual, axis=-1))
    weight = live_flags[:, None, None] * threshold / jnp.maximum(row_norms, threshold)
    scaled = (weight[..., None] * residual).astype(jnp.bfloat16)
    return (scaled, weight.astype(jnp.bfloat16))


def body(design_tiles, block_ids, responses, live_groups, start_coef):
    row_place = lax.axis_index("row")
    feat_place = lax.axis_index("feat")
    block_width = design_tiles.shape[-1]
    columns = start_coef.shape[1]
    local_blocks = start_coef.shape[0] // block_width
    local_ids = block_ids - feat_place * local_blocks
    work_tiles = design_tiles[0]
    work_resp = responses[0]
    work_ids = lax.dynamic_index_in_dim(local_ids, row_place, 0, keepdims=False)
    live_flags = lax.dynamic_index_in_dim(live_groups, row_place, 0, keepdims=False).astype(
        jnp.float32
    )
    onehot = (
        work_ids.reshape(-1)[:, None] == jnp.arange(local_blocks, dtype=jnp.int32)[None, :]
    ).astype(jnp.float32)
    tiles_wide = work_tiles.astype(jnp.float32)
    tile_squares = tiles_wide * tiles_wide
    coefficients = start_coef
    for iteration in range(ITERS):
        coef_bf = coefficients.astype(jnp.bfloat16).reshape(local_blocks, block_width, columns)
        picked = coef_bf[work_ids]
        predicted = jnp.einsum(
            "gskif,gskfc->gsic", work_tiles, picked, preferred_element_type=jnp.float32
        )
        scaled, rounded = huber_weights(predicted, work_resp, live_flags)
        partial_grad = jnp.einsum(
            "gskif,gsic->gskfc", work_tiles, scaled, preferred_element_type=jnp.float32
        )
        partial_curv = jnp.einsum(
            "gskif,gsi->gskf",
            tile_squares,
            rounded.astype(jnp.float32),
            precision=lax.Precision.HIGHEST,
        )
        gradient = jnp.einsum(
            "tb,tfc->bfc",
            onehot,
            partial_grad.reshape(-1, block_width, columns),
            precision=lax.Precision.HIGHEST,
        )
        curvature = jnp.einsum(
            "tb,tf->bf",
            onehot,
            partial_curv.reshape(-1, block_width),
            precision=lax.Precision.HIGHEST,
        )
        gradient, curvature = lax.psum((gradient, curvature), "row")
        coefficients = coefficients + step_size * (
            gradient.reshape(-1, columns) - ridge_term * coefficients
        ) / (curvature.reshape(-1, 1) + ridge_term)
    return coefficients


def solution(mesh):
    in_specs = (
        P("row", None, None, "feat", None, None),
        P(None, None, None, "feat"),
        P("row", None, None, None, None),
        P(),
        P("feat", None),
    )
    out_specs = P("feat", None)
    return jax.shard_map(body, mesh=mesh, in_specs=in_specs, out_specs=out_specs, check_vma=False)
```

profile of v0, /device:TPU:0, one launch (start us, length us, event | category | flops | bytes accessed | tf_op | source)
XLA Modules:
  0.0 509.8 jit_solution(7656828350380415054)
XLA Ops:
  6.5 0.7 compare_select_fusion
  7.5 1.9 copy_bitcast_fusion.3
  9.4 2.7 gather_fusion
  12.1 8.0 %fusion.16 = f32[8,8,128,64]{2,3,1,0:T(8,128)} fusion(bf16[8,8,3,128,64]{3,4,2,1,0:T(8,128)(2,1)} %bitcast.118, bf16[1,8,8,3,128,128]{5,4,3,2,1,0:T(8,128)(2,1)} %param.5), kind=kOutput, calls=%fused_computation.29 | convolution fusion | flops 402653184 | bytes 11534336 | tf_op jit(solution)/shard_map/gskif,gskfc->gsic/dot_general | solution.py:44
  21.3 124.6 %all-reduce.5.cloned.1.call-done = f32[8,8,128,64]{2,3,1,0:T(8,128)} async-done(((f32[8,8,128,64]{2,3,1,0:T(8,128)}), f32[8,8,128,64]{2,3,1,0:T(8,128)}) %all-reduce.5.cloned.1.call-update) | async-done | bytes 2097168 | tf_op jit(solution)/shard_map/psum | solution.py:14
  146.0 2.2 multiply_reduce_fusion.1
  148.2 4.1 fusion.8
  152.3 6.2 %fusion.14 = f32[64,128,64]{1,0,2:T(8,128)S(1)} fusion(f32[192,128,64]{1,2,0:T(8,128)S(1)} %bitcast.115, s32[192]{0:T(256)S(1)} %eq.15), kind=kOutput, calls=%fused_computation.17 | convolution fusion | flops 1207971840 | bytes 8389376 | tf_op jit(solution)/shard_map/tb,tfc->bfc/dot_general | solution.py:57
  158.5 2.5 copy.46
  161.3 7.4 %fusion.1 = f32[8,8,1,3,128]{4,2,3,1,0:T(1,128)S(1)} fusion(bf16[1,8,8,3,128,128]{5,4,3,2,1,0:T(8,128)(2,1)} %param.5, bf16[8,8,128,1,1]{2,1,0,3,4:T(8,128)(2,1)S(1)} %get-tuple-element.7), kind=kOutput, calls=%fused_computation.4 | convolution fusion | flops 44040192 | bytes 6406144 | tf_op jit(solution)/shard_map/gskif,gsi->gskf/dot_general | solution.py:51
  169.0 41.4 %psum.44 = f32[64,128]{1,0:T(8,128)S(1)} all-reduce(f32[64,128]{1,0:T(8,128)S(1)} %fusion.31), channel_id=1, replica_groups=mesh['row'=8,'feat'=16] {'row'}, use_global_device_ids=true, to_apply=%region_3.4 | all-reduce | flops 8192 | bytes 65536 | tf_op jit(solution)/shard_map/psum | solution.py:69
  210.4 44.2 %all-reduce.7.cloned.1.call-done = f32[8192,64]{0,1:T(8,128)} async-done(((f32[8192,64]{0,1:T(8,128)}), f32[8192,64]{0,1:T(8,128)}) %all-reduce.7.cloned.1.call-update) | async-done | bytes 2097168 | tf_op jit(solution)/shard_map/psum | solution.py:69
  254.6 2.7 copy_bitcast_fusion.2
  257.3 2.7 gather_fusion.1
  260.0 8.0 %fusion.19 = f32[8,8,128,64]{2,3,1,0:T(8,128)} fusion(bf16[8,8,3,128,64]{3,4,2,1,0:T(8,128)(2,1)} %bitcast.117, bf16[1,8,8,3,128,128]{5,4,3,2,1,0:T(8,128)(2,1)} %param.5), kind=kOutput, calls=%fused_computation.30 | convolution fusion | flops 402653184 | bytes 11534336 | tf_op jit(solution)/shard_map/gskif,gskfc->gsic/dot_general | solution.py:44
  268.3 122.0 %all-reduce.9.cloned.1.call-done = f32[8,8,128,64]{2,3,1,0:T(8,128)} async-done(((f32[8,8,128,64]{2,3,1,0:T(8,128)}), f32[8,8,128,64]{2,3,1,0:T(8,128)}) %all-reduce.9.cloned.1.call-update) | async-done | bytes 2097168 | tf_op jit(solution)/shard_map/psum | solution.py:14
  390.3 2.2 multiply_reduce_fusion
  392.5 4.1 fusion.3
  396.6 6.2 %fusion.12 = f32[64,128,64]{1,0,2:T(8,128)S(1)} fusion(f32[192,128,64]{1,2,0:T(8,128)S(1)} %bitcast.116, s32[192]{0:T(256)S(1)} %eq.15), kind=kOutput, calls=%fused_computation.15 | convolution fusion | flops 1207971840 | bytes 8389376 | tf_op jit(solution)/shard_map/tb,tfc->bfc/dot_general | solution.py:57
  402.8 2.5 copy.45
  405.4 7.8 %fusion = f32[8,8,1,3,128]{4,2,3,1,0:T(1,128)S(1)} fusion(bf16[1,8,8,3,128,128]{5,4,3,2,1,0:T(8,128)(2,1)} %param.5, bf16[8,8,128,1,1]{2,1,0,3,4:T(8,128)(2,1)S(1)} %get-tuple-element.5), kind=kOutput, calls=%fused_computation.3 | convolution fusion | flops 44040192 | bytes 6406144 | tf_op jit(solution)/shard_map/gskif,gsi->gskf/dot_general | solution.py:51
  413.5 41.4 %psum.47 = f32[64,128]{1,0:T(8,128)S(1)} all-reduce(f32[64,128]{1,0:T(8,128)S(1)} %fusion.30), channel_id=1, replica_groups=mesh['row'=8,'feat'=16] {'row'}, use_global_device_ids=true, to_apply=%region_7.8 | all-reduce | flops 8192 | bytes 65536 | tf_op jit(solution)/shard_map/psum | solution.py:69
  454.9 44.2 %all-reduce.11.cloned.1.call-done = f32[8192,64]{0,1:T(8,128)} async-done(((f32[8192,64]{0,1:T(8,128)}), f32[8192,64]{0,1:T(8,128)}) %all-reduce.11.cloned.1.call-update) | async-done | bytes 2097168 | tf_op jit(solution)/shard_map/psum | solution.py:69
  499.1 4.2 divide_add_fusion
  (32 shorter events, 2.8 us)
Async XLA Ops:
  6.5 139.4 %all-reduce.5.cloned.1.call-start = ((), (), s32[]{:S(2)}) async-start(), calls=%async_computation | async-start | bytes 4194304 | tf_op jit(solution)/shard_map/psum | solution.py:14
  20.1 125.9 %copy-start = (bf16[1,8,8,128,64]{3,4,2,1,0:T(8,128)(2,1)S(1)}, bf16[1,8,8,128,64]{3,4,2,1,0:T(8,128)(2,1)}, u32[]{:S(2)}) copy-start(bf16[1,8,8,128,64]{3,4,2,1,0:T(8,128)(2,1)} %param.7) | copy-start | bytes 3145732
  20.1 234.5 %all-reduce.7.cloned.1.call-start = ((), (), s32[]{:S(2)}) async-start(), calls=%async_computation.1 | async-start | bytes 4194304 | tf_op jit(solution)/shard_map/psum | solution.py:69
  146.0 2.3 copy-start.2
  161.1 229.2 %all-reduce.9.cloned.1.call-start = ((), (), s32[]{:S(2)}) async-start(), calls=%async_computation.2 | async-start | bytes 4194304 | tf_op jit(solution)/shard_map/psum | solution.py:14
  268.0 231.1 %all-reduce.11.cloned.1.call-start = ((), (), s32[]{:S(2)}) async-start(), calls=%async_computation.3 | async-start | bytes 4194304 | tf_op jit(solution)/shard_map/psum | solution.py:69
  390.3 2.3 copy-start.3
  405.4 93.7 %copy-start.1 = (f32[8192,64]{0,1:T(8,128)S(1)}, f32[8192,64]{0,1:T(8,128)}, u32[]{:S(2)}) copy-start(f32[8192,64]{0,1:T(8,128)} %param.9) | copy-start | bytes 6291460
Sparse Core Ops, SparseCore 0:
  20.2 125.6 all-reduce.4
  161.2 93.3 all-reduce.6
  268.1 122.1 all-reduce.8
  405.5 93.5 all-reduce.10
where the time goes:
time: 510 us
  waiting for transfers between devices  335 us (66%)
  blocking collectives  82.7 us (16%)
  matrix products  52.1 us (10%)
  other arithmetic  14.8 us (3%)
  between operations  13.2 us (3%)
  local copies, waits for them, and re-layouts  11.2 us (2%)
    psum x2, waiting for transfers between devices, huber_weights(): totals = lax.psum(predicted, 'feat')  247 us
    psum x2, waiting for transfers between devices, body(): gradient, curvature = lax.psum((gradient, curvature), 'row')  88.4 us
    psum x2, blocking collectives, body(): gradient, curvature = lax.psum((gradient, curvature), 'row')  82.7 us
    dot_general x2, matrix products, body(): jnp.einsum('gskif,gskfc->gsic', work_tiles, picked, preferred_element_typ...  15.9 us
    dot_general x2, matrix products, body(): jnp.einsum('gskif,gsi->gskf', tile_squares, rounded.astype(jnp.float32),...  15.2 us
    dot_general x2, matrix products, body(): jnp.einsum('tb,tfc->bfc', onehot, partial_grad.reshape(-1, block_width, c...  12.4 us
  transfers between devices with their start and end apart: 4, of which 4 were waited for; matrix products, arithmetic and copies ran while one was open for 3% of the time, Pallas kernels for 0%

commit v1 on v0

--- a/solution.py
+++ b/solution.py
@@ -11,7 +11,7 @@
 def huber_weights(predicted, work_resp, live_flags):
     groups, slot_count, block_rows, columns = predicted.shape
     threshold = 1.4 * columns**0.5
-    totals = lax.psum(predicted, "feat")
+    totals = jnp.sum(lax.all_gather(predicted, "feat"), axis=0)
     residual = work_resp.astype(jnp.float32) - totals
     row_norms = jnp.sqrt(jnp.sum(residual * residual, axis=-1))
     weight = live_flags[:, None, None] * threshold / jnp.maximum(row_norms, threshold)

time: 510 us -> 632 us (1.24)
  waiting for transfers between devices: 335 us -> 430 us
  other arithmetic: 14.8 us -> 41.6 us
    all_gather x0 -> x2, waiting for transfers between devices: none -> 341 us  [huber_weights(): totals = jnp.sum(lax.all_gather(predicted, 'feat'), axis=0)]
    psum x2 -> x0, waiting for transfers between devices: 247 us -> none  [huber_weights(): totals = lax.psum(predicted, 'feat')]
    reduce_sum x0 -> x2, other arithmetic: none -> 26.9 us  [huber_weights(): totals = jnp.sum(lax.all_gather(predicted, 'feat'), axis=0)]
where the time goes in v1:
time: 632 us
  waiting for transfers between devices  430 us (68%)
  blocking collectives  83.3 us (13%)
  matrix products  52.1 us (8%)
  other arithmetic  41.6 us (7%)
  between operations  13.2 us (2%)
  local copies, waits for them, and re-layouts  11.2 us (2%)
    all_gather x2, waiting for transfers between devices, huber_weights(): totals = jnp.sum(lax.all_gather(predicted, 'feat'), axis=0)  341 us
    psum x2, waiting for transfers between devices, body(): gradient, curvature = lax.psum((gradient, curvature), 'row')  88 us
    psum x2, blocking collectives, body(): gradient, curvature = lax.psum((gradient, curvature), 'row')  83.3 us
    reduce_sum x2, other arithmetic, huber_weights(): totals = jnp.sum(lax.all_gather(predicted, 'feat'), axis=0)  26.9 us
    dot_general x2, matrix products, body(): jnp.einsum('gskif,gskfc->gsic', work_tiles, picked, preferred_element_typ...  15.9 us
    dot_general x2, matrix products, body(): jnp.einsum('gskif,gsi->gskf', tile_squares, rounded.astype(jnp.float32),...  15.2 us
  transfers between devices with their start and end apart: 4, of which 4 were waited for; matrix products, arithmetic and copies ran while one was open for 3% of the time, Pallas kernels for 0%

profile of v1, /device:TPU:0, one launch (start us, length us, event | category | flops | bytes accessed | tf_op | source)
XLA Modules:
  0.0 631.8 jit_solution(385102591174954676)
XLA Ops:
  9.4 2.7 gather_fusion
  12.1 8.0 %fusion.16 = f32[8,8,128,64]{2,3,1,0:T(8,128)} fusion(bf16[8,8,3,128,64]{3,4,2,1,0:T(8,128)(2,1)} %bitcast.122, bf16[1,8,8,3,128,128]{5,4,3,2,1,0:T(8,128)(2,1)} %param.5), kind=kOutput, calls=%fused_computation.29 | convolution fusion | flops 402653184 | bytes 11534336 | tf_op jit(solution)/shard_map/gskif,gskfc->gsic/dot_general | solution.py:44
  21.3 172.1 %all-gather.5.cloned.1.call-done = f32[128,8,128,64]{2,3,1,0:T(8,128)} async-done(((f32[8,8,128,64]{2,3,1,0:T(8,128)}), f32[128,8,128,64]{2,3,1,0:T(8,128)}) %all-gather.5.cloned.1.call-update) | async-done | bytes 33554448 | tf_op jit(solution)/shard_map/all_gather | solution.py:14
  193.4 13.5 %reduce_sum.36 = f32[8,8,128,64]{2,3,1,0:T(8,128)} reduce(f32[16,8,8,128,64]{3,4,2,1,0:T(8,128)} %bitcast.119, f32[]{:T(128)} %constant.17.clone.1), dimensions={0}, to_apply=%region_0.1 | reduce | flops 7864320 | bytes 35651588 | tf_op jit(solution)/shard_map/reduce_sum | solution.py:14
  206.9 2.2 multiply_reduce_fusion.1
  209.1 4.1 fusion.8
  213.2 6.2 fusion.14
  219.4 2.5 copy.52
  222.2 7.4 %fusion.1 = f32[8,8,1,3,128]{4,2,3,1,0:T(1,128)S(1)} fusion(bf16[1,8,8,3,128,128]{5,4,3,2,1,0:T(8,128)(2,1)} %param.5, bf16[8,8,128,1,1]{2,1,0,3,4:T(8,128)(2,1)S(1)} %get-tuple-element.7), kind=kOutput, calls=%fused_computation.4 | convolution fusion | flops 44040192 | bytes 6406144 | tf_op jit(solution)/shard_map/gskif,gsi->gskf/dot_general | solution.py:51
  229.9 41.7 %psum.29 = f32[64,128]{1,0:T(8,128)S(1)} all-reduce(f32[64,128]{1,0:T(8,128)S(1)} %fusion.31), channel_id=1, replica_groups=mesh['row'=8,'feat'=16] {'row'}, use_global_device_ids=true, to_apply=%region_3.4 | all-reduce | flops 8192 | bytes 65536 | tf_op jit(solution)/shard_map/psum | solution.py:69
  271.6 44.1 %all-reduce.3.cloned.1.call-done = f32[8192,64]{0,1:T(8,128)} async-done(((f32[8192,64]{0,1:T(8,128)}), f32[8192,64]{0,1:T(8,128)}) %all-reduce.3.cloned.1.call-update) | async-done | bytes 2097168 | tf_op jit(solution)/shard_map/psum | solution.py:69
  315.7 2.7 copy_bitcast_fusion.2
  318.4 2.7 gather_fusion.1
  321.1 8.0 %fusion.19 = f32[8,8,128,64]{2,3,1,0:T(8,128)} fusion(bf16[8,8,3,128,64]{3,4,2,1,0:T(8,128)(2,1)} %bitcast.121, bf16[1,8,8,3,128,128]{5,4,3,2,1,0:T(8,128)(2,1)} %param.5), kind=kOutput, calls=%fused_computation.30 | convolution fusion | flops 402653184 | bytes 11534336 | tf_op jit(solution)/shard_map/gskif,gskfc->gsic/dot_general | solution.py:44
  329.4 169.4 %all-gather.7.cloned.1.call-done = f32[128,8,128,64]{2,3,1,0:T(8,128)} async-done(((f32[8,8,128,64]{2,3,1,0:T(8,128)}), f32[128,8,128,64]{2,3,1,0:T(8,128)}) %all-gather.7.cloned.1.call-update) | async-done | bytes 33554448 | tf_op jit(solution)/shard_map/all_gather | solution.py:14
  498.8 13.4 %reduce_sum.38 = f32[8,8,128,64]{2,3,1,0:T(8,128)} reduce(f32[16,8,8,128,64]{3,4,2,1,0:T(8,128)} %bitcast.120, f32[]{:T(128)} %constant.17.clone.1), dimensions={0}, to_apply=%region_4.5 | reduce | flops 7864320 | bytes 35651588 | tf_op jit(solution)/shard_map/reduce_sum | solution.py:14
  512.2 2.2 multiply_reduce_fusion
  514.5 4.1 fusion.3
  518.6 6.2 fusion.12
  524.8 2.5 copy.51
  527.3 7.8 %fusion = f32[8,8,1,3,128]{4,2,3,1,0:T(1,128)S(1)} fusion(bf16[1,8,8,3,128,128]{5,4,3,2,1,0:T(8,128)(2,1)} %param.5, bf16[8,8,128,1,1]{2,1,0,3,4:T(8,128)(2,1)S(1)} %get-tuple-element.5), kind=kOutput, calls=%fused_computation.3 | convolution fusion | flops 44040192 | bytes 6406144 | tf_op jit(solution)/shard_map/gskif,gsi->gskf/dot_general | solution.py:51
  535.5 41.7 %psum.31 = f32[64,128]{1,0:T(8,128)S(1)} all-reduce(f32[64,128]{1,0:T(8,128)S(1)} %fusion.30), channel_id=1, replica_groups=mesh['row'=8,'feat'=16] {'row'}, use_global_device_ids=true, to_apply=%region_7.8 | all-reduce | flops 8192 | bytes 65536 | tf_op jit(solution)/shard_map/psum | solution.py:69
  577.1 43.9 %all-reduce.5.cloned.1.call-done = f32[8192,64]{0,1:T(8,128)} async-done(((f32[8192,64]{0,1:T(8,128)}), f32[8192,64]{0,1:T(8,128)}) %all-reduce.5.cloned.1.call-update) | async-done | bytes 2097168 | tf_op jit(solution)/shard_map/psum | solution.py:69
  621.0 4.2 divide_add_fusion
  (34 shorter events, 5.4 us)
Async XLA Ops:
  6.5 186.8 %all-gather.5.cloned.1.call-start = ((), (), s32[]{:S(2)}) async-start(), calls=%async_computation.2 | async-start | bytes 35651584 | tf_op jit(solution)/shard_map/all_gather | solution.py:14
  20.1 295.6 %all-reduce.3.cloned.1.call-start = ((), (), s32[]{:S(2)}) async-start(), calls=%async_computation | async-start | bytes 4194304 | tf_op jit(solution)/shard_map/psum | solution.py:69
  193.4 13.5 %copy-start = (bf16[1,8,8,128,64]{3,4,2,1,0:T(8,128)(2,1)S(1)}, bf16[1,8,8,128,64]{3,4,2,1,0:T(8,128)(2,1)}, u32[]{:S(2)}) copy-start(bf16[1,8,8,128,64]{3,4,2,1,0:T(8,128)(2,1)} %param.7) | copy-start | bytes 3145732
  206.9 2.3 copy-start.2
  222.0 276.9 %all-gather.7.cloned.1.call-start = ((), (), s32[]{:S(2)}) async-start(), calls=%async_computation.3 | async-start | bytes 35651584 | tf_op jit(solution)/shard_map/all_gather | solution.py:14
  329.1 291.9 %all-reduce.5.cloned.1.call-start = ((), (), s32[]{:S(2)}) async-start(), calls=%async_computation.1 | async-start | bytes 4194304 | tf_op jit(solution)/shard_map/psum | solution.py:69
  512.2 2.3 copy-start.1
  527.3 93.7 %copy-start.3 = (f32[8192,64]{0,1:T(8,128)S(1)}, f32[8192,64]{0,1:T(8,128)}, u32[]{:S(2)}) copy-start(f32[8192,64]{0,1:T(8,128)} %param.9) | copy-start | bytes 6291460
Sparse Core Ops, SparseCore 0:
  20.2 173.0 all-gather.4
  222.1 93.5 all-reduce.2
  329.2 169.5 all-gather.6
  527.4 93.5 all-reduce.4
